TPU v7x, 32 devices: a whole 2x2x4 slice. The times are simulated.
32 devices in a mesh: row: 4 (over z), col: 4 (over y, x), ka: 2 (over core).
Axes of the slice: x: 2, y: 2, z: 4, core: 2. Of those that a mesh axis runs over, the one named last changes fastest.
Arguments:
- iterate: float32 [2560, 13824], P('row', ('col', 'ka')), may hold values from -0.03125 to 0.03125
Outputs:
- update: bfloat16 [2560, 13824], P('row', ('col', 'ka'))
All inputs are finite; a program needn't handle non-finite values.
Results may differ from a plain program's by a relative error of at most 0.02.
Values may be sent and summed in bfloat16 or wider, within the bound.
A program may use at most 64 MiB of HBM per device.

v0:
```python
import math

import jax
import jax.numpy as jnp
from jax import lax
from jax.sharding import PartitionSpec as P

K = 13824
ITERS = 2


LINEAR_COEF = 3.4445
CUBIC_COEF = -4.775
QUINTIC_COEF = 2.0315


def body(iterate):
    current = iterate
    for step in range(ITERS):
        rounded = current.astype(jnp.bfloat16)
        gathered = lax.all_gather(rounded, "row", axis=0, tiled=True)
        block = lax.psum_scatter(
            lax.dot_general(
                gathered, rounded, (((1,), (1,)), ((), ())), preferred_element_type=jnp.float32
            ),
            ("col", "ka"),
            scatter_dimension=0,
            tiled=True,
        )
        panel = lax.all_gather(block.astype(jnp.bfloat16), ("col", "ka"), axis=0, tiled=True)
        first = lax.dot_general(
            panel, gathered, (((0,), (0,)), ((), ())), preferred_element_type=jnp.float32
        ).astype(jnp.bfloat16)
        second = lax.dot_general(
            panel,
            lax.all_gather(first, "row", axis=0, tiled=True),
            (((0,), (0,)), ((), ())),
            preferred_element_type=jnp.float32,
        )
        current = (
            LINEAR_COEF * current + CUBIC_COEF * first.astype(jnp.float32) + QUINTIC_COEF * second
        )
    return (math.sqrt(K) * current).astype(jnp.bfloat16)


def solution(mesh):
    in_specs = (P("row", ("col", "ka")),)
    out_specs = P("row", ("col", "ka"))
    return jax.shard_map(body, mesh=mesh, in_specs=in_specs, out_specs=out_specs, check_vma=False)
```

profile of v0, /device:TPU:0, one launch (start us, length us, event | category | flops | bytes accessed | tf_op | source)
XLA Modules:
  0.0 916.1 jit_solution(5216039706412930454)
XLA Ops:
  6.5 3.8 convert_element_type.27
  10.4 0.0 all-gather.7.cloned.1.call-update
  10.4 0.0 reduce-scatter.3.cloned.1.call-start
  10.5 159.9 %all-gather.7.cloned.1.call-done = bf16[2560,1728]{0,1:T(8,128)(2,1)} async-done(((bf16[640,1728]{0,1:T(8,128)(2,1)}), bf16[2560,1728]{0,1:T(8,128)(2,1)}) %all-gather.7.cloned.1.call-update) | async-done | bytes 8847376 | tf_op jit(solution)/shard_map/all_gather | solution.py:21
  170.4 12.3 %fusion.1 = f32[2560,640]{1,0:T(8,128)} fusion(bf16[2560,1728]{0,1:T(8,128)(2,1)} %all-gather.7.cloned.1.call-done, bf16[640,1728]{0,1:T(8,128)(2,1)} %convert_element_type.27), kind=kOutput, calls=%fused_computation.5 | convolution fusion | flops 5662310400 | bytes 17612800 | tf_op jit(solution)/shard_map/dot_general | solution.py:23
  182.7 0.0 reduce-scatter.3.cloned.1.call-update
  182.7 0.0 all-gather.9.cloned.1.call-start
  182.7 61.3 %reduce-scatter.3.cloned.1.call-done = f32[320,640]{1,0:T(8,128)} async-done(((f32[2560,640]{1,0:T(8,128)}), f32[320,640]{1,0:T(8,128)}) %reduce-scatter.3.cloned.1.call-update) | async-done | bytes 819216 | tf_op jit(solution)/shard_map/reduce_scatter | solution.py:22
  244.0 1.9 convert_element_type.28
  246.0 0.0 all-gather.9.cloned.1.call-update
  246.0 0.0 all-gather.11.cloned.1.call-start
  246.1 32.9 %all-gather.9.cloned.1.call-done = bf16[2560,640]{1,0:T(8,128)(2,1)} async-done(((bf16[320,640]{1,0:T(8,128)(2,1)}), bf16[2560,640]{1,0:T(8,128)(2,1)}) %all-gather.9.cloned.1.call-update) | async-done | bytes 3276816 | tf_op jit(solution)/shard_map/all_gather | solution.py:30
  279.0 12.4 %convolution_convert_fusion.1 = bf16[640,1728]{0,1:T(8,128)(2,1)} fusion(bf16[2560,1728]{0,1:T(8,128)(2,1)} %all-gather.7.cloned.1.call-done, bf16[2560,640]{1,0:T(8,128)(2,1)} %all-gather.9.cloned.1.call-done), kind=kOutput, calls=%fused_computation.3 | convolution fusion | flops 5663416320 | bytes 14336000 | tf_op jit(solution)/shard_map/dot_general | solution.py:31
  291.4 0.0 all-gather.11.cloned.1.call-update
  291.5 0.0 all-gather.13.cloned.1.call-start
  291.5 157.2 %all-gather.11.cloned.1.call-done = bf16[2560,1728]{0,1:T(8,128)(2,1)} async-done(((bf16[640,1728]{0,1:T(8,128)(2,1)}), bf16[2560,1728]{0,1:T(8,128)(2,1)}) %all-gather.11.cloned.1.call-update) | async-done | bytes 8847376 | tf_op jit(solution)/shard_map/all_gather | solution.py:36
  448.8 13.4 %fusion = (bf16[640,1728]{0,1:T(8,128)(2,1)}, f32[640,1728]{0,1:T(8,128)}) fusion(bf16[2560,1728]{0,1:T(8,128)(2,1)} %all-gather.11.cloned.1.call-done, bf16[2560,640]{1,0:T(8,128)(2,1)S(1)} %copy-done, bf16[640,1728]{0,1:T(8,128)(2,1)} %convolution_convert_fusion.1, f32[640,1728]{0,1:T(8,128)} %param.1), kind=kOutput, calls=%fused_computation.4 | convolution fusion | flops 5670051840 | bytes 25395200 | tf_op jit(solution)/shard_map/dot_general | solution.py:34
  462.2 0.0 all-gather.13.cloned.1.call-update
  462.2 0.2 reduce-scatter.5.cloned.1.call-start
  462.4 155.3 %all-gather.13.cloned.1.call-done = bf16[2560,1728]{0,1:T(8,128)(2,1)} async-done(((bf16[640,1728]{0,1:T(8,128)(2,1)}), bf16[2560,1728]{0,1:T(8,128)(2,1)}) %all-gather.13.cloned.1.call-update) | async-done | bytes 8847376 | tf_op jit(solution)/shard_map/all_gather | solution.py:21
  617.7 12.3 %fusion.2 = f32[2560,640]{1,0:T(8,128)} fusion(bf16[2560,1728]{0,1:T(8,128)(2,1)} %all-gather.13.cloned.1.call-done, bf16[640,1728]{0,1:T(8,128)(2,1)} %get-tuple-element.5), kind=kOutput, calls=%fused_computation.6 | convolution fusion | flops 5662310400 | bytes 17612800 | tf_op jit(solution)/shard_map/dot_general | solution.py:23
  630.0 0.0 reduce-scatter.5.cloned.1.call-update
  630.0 0.0 all-gather.15.cloned.1.call-start
  630.0 61.3 %reduce-scatter.5.cloned.1.call-done = f32[320,640]{1,0:T(8,128)} async-done(((f32[2560,640]{1,0:T(8,128)}), f32[320,640]{1,0:T(8,128)}) %reduce-scatter.5.cloned.1.call-update) | async-done | bytes 819216 | tf_op jit(solution)/shard_map/reduce_scatter | solution.py:22
  691.3 1.9 convert_element_type.32
  693.3 0.0 all-gather.15.cloned.1.call-update
  693.3 0.0 all-gather.17.cloned.1.call-start
  693.4 32.9 %all-gather.15.cloned.1.call-done = bf16[2560,640]{1,0:T(8,128)(2,1)} async-done(((bf16[320,640]{1,0:T(8,128)(2,1)}), bf16[2560,640]{1,0:T(8,128)(2,1)}) %all-gather.15.cloned.1.call-update) | async-done | bytes 3276816 | tf_op jit(solution)/shard_map/all_gather | solution.py:30
  726.3 12.4 %convolution_convert_fusion = bf16[640,1728]{0,1:T(8,128)(2,1)} fusion(bf16[2560,1728]{0,1:T(8,128)(2,1)} %all-gather.13.cloned.1.call-done, bf16[2560,640]{1,0:T(8,128)(2,1)} %all-gather.15.cloned.1.call-done), kind=kOutput, calls=%fused_computation.2 | convolution fusion | flops 5663416320 | bytes 14336000 | tf_op jit(solution)/shard_map/dot_general | solution.py:31
  738.7 0.0 all-gather.17.cloned.1.call-update
  738.8 157.3 %all-gather.17.cloned.1.call-done = bf16[2560,1728]{0,1:T(8,128)(2,1)} async-done(((bf16[640,1728]{0,1:T(8,128)(2,1)}), bf16[2560,1728]{0,1:T(8,128)(2,1)}) %all-gather.17.cloned.1.call-update) | async-done | bytes 8847376 | tf_op jit(solution)/shard_map/all_gather | solution.py:36
  896.1 13.3 %multiply_convert_fusion = bf16[640,1728]{0,1:T(8,128)(2,1)} fusion(bf16[640,1728]{0,1:T(8,128)(2,1)} %convolution_convert_fusion, f32[640,1728]{0,1:T(8,128)} %get-tuple-element.6, bf16[2560,1728]{0,1:T(8,128)(2,1)} %all-gather.17.cloned.1.call-done, bf16[2560,640]{1,0:T(8,128)(2,1)S(1)} %copy-done.1), kind=kOutput, calls=%fused_computation | convolution fusion | flops 5671157760 | bytes 20971520 | tf_op jit(solution)/shard_map/dot_general | solution.py:34
  (5 shorter events, 0.0 us)
Async XLA Ops:
  6.5 163.9 %all-gather.7.cloned.1.call-start = ((), (), s32[]{:S(2)}) async-start(), calls=%async_computation.2 | async-start | bytes 11059200 | tf_op jit(solution)/shard_map/all_gather | solution.py:21
  10.4 233.6 %reduce-scatter.3.cloned.1.call-start = ((), (), s32[]{:S(2)}) async-start(), calls=%async_computation.3 | async-start | bytes 7372800 | tf_op jit(solution)/shard_map/reduce_scatter | solution.py:22
  182.7 96.3 %all-gather.9.cloned.1.call-start = ((), (), s32[]{:S(2)}) async-start(), calls=%async_computation.4 | async-start | bytes 3686400 | tf_op jit(solution)/shard_map/all_gather | solution.py:30
  246.0 202.7 %all-gather.11.cloned.1.call-start = ((), (), s32[]{:S(2)}) async-start(), calls=%async_computation.5 | async-start | bytes 11059200 | tf_op jit(solution)/shard_map/all_gather | solution.py:36
  279.0 169.7 %copy-start = (bf16[2560,640]{1,0:T(8,128)(2,1)S(1)}, bf16[2560,640]{1,0:T(8,128)(2,1)}, u32[]{:S(2)}) copy-start(bf16[2560,640]{1,0:T(8,128)(2,1)} %all-gather.9.cloned.1.call-done) | copy-start | bytes 9830404
  291.5 326.2 %all-gather.13.cloned.1.call-start = ((), (), s32[]{:S(2)}) async-start(), calls=%async_computation.6 | async-start | bytes 11059200 | tf_op jit(solution)/shard_map/all_gather | solution.py:21
  462.2 229.1 %reduce-scatter.5.cloned.1.call-start = ((), (), s32[]{:S(2)}) async-start(), calls=%async_computation.7 | async-start | bytes 7372800 | tf_op jit(solution)/shard_map/reduce_scatter | solution.py:22
  630.0 96.3 %all-gather.15.cloned.1.call-start = ((), (), s32[]{:S(2)}) async-start(), calls=%async_computation.8 | async-start | bytes 3686400 | tf_op jit(solution)/shard_map/all_gather | solution.py:30
  693.3 202.7 %all-gather.17.cloned.1.call-start = ((), (), s32[]{:S(2)}) async-start(), calls=%async_computation.9 | async-start | bytes 11059200 | tf_op jit(solution)/shard_map/all_gather | solution.py:36
  726.3 169.7 %copy-start.1 = (bf16[2560,640]{1,0:T(8,128)(2,1)S(1)}, bf16[2560,640]{1,0:T(8,128)(2,1)}, u32[]{:S(2)}) copy-start(bf16[2560,640]{1,0:T(8,128)(2,1)} %all-gather.15.cloned.1.call-done) | copy-start | bytes 9830404
Sparse Core Ops, SparseCore 0:
  10.5 159.8 all-gather.6
  182.8 61.1 reduce-scatter.2
  246.1 32.8 all-gather.8
  291.6 157.1 all-gather.10
  462.3 155.3 all-gather.12
  630.1 61.1 reduce-scatter.4
  693.4 32.8 all-gather.14
  738.9 157.1 all-gather.16
where the time goes:
time: 916 us
  waiting for transfers between devices  818 us (89%)
  matrix products  76.1 us (8%)
  between operations  13.5 us (1%)
    all_gather x2, waiting for transfers between devices, body(): gathered = lax.all_gather(rounded, 'row', axis=0, tiled=True)  315 us
    all_gather x2, waiting for transfers between devices, body(): lax.all_gather(first, 'row', axis=0, tiled=True)  315 us
    reduce_scatter x2, waiting for transfers between devices, body(): lax.psum_scatter(lax.dot_general(gathered, rounded, (((1,), (1,)), ((), (...  123 us
    all_gather x2, waiting for transfers between devices, body(): lax.all_gather(block.astype(jnp.bfloat16), ('col', 'ka'), axis=0, tiled=T...  65.9 us
    dot_general x2, matrix products, body(): lax.dot_general(panel, lax.all_gather(first, 'row', axis=0, tiled=True),...  26.7 us
    dot_general x2, matrix products, body(): lax.dot_general(panel, gathered, (((0,), (0,)), ((), ())), preferred_elem...  24.9 us
    dot_general x2, matrix products, body(): lax.dot_general(gathered, rounded, (((1,), (1,)), ((), ())), preferred_el...  24.5 us
  transfers between devices with their start and end apart: 8, of which 8 were waited for; matrix products, arithmetic and copies ran while one was open for 0% of the time, Pallas kernels for 0%

commit v1 on v0

v1 whole, which is shorter than its diff:
```python
import functools
import math

import jax
import jax.numpy as jnp
from jax import lax
from jax.experimental import pallas as pl
from jax.experimental.pallas import tpu as pltpu
from jax.sharding import PartitionSpec as P

LINEAR_COEF = 3.4445
CUBIC_COEF = -4.775
QUINTIC_COEF = 2.0315

MESH = pl.DeviceIdType.MESH


def tile_of(size, most):
    return max(t for t in range(16, min(size, most) + 1, 16) if size % t == 0)


def shifted(value, diagonal, rows, columns):
    r = lax.broadcasted_iota(jnp.int32, value.shape, 0) + rows
    c = lax.broadcasted_iota(jnp.int32, value.shape, 1) + columns
    return value + jnp.where(r == c, jnp.float32(diagonal), jnp.float32(0.0))


def polynomial_kernel(
    mine, u_ref, q_ref, g_ref, p_ref, g1_ref, b_ref, p1_ref, u_sem, p_send, p_recv, g_send, g_recv, q_sems
):
    n = g_ref.shape[0]
    half = n // 2
    columns = tile_of(n, 256)
    steps = n // columns
    ka = lax.axis_index("ka")
    other = {"ka": 1 - ka}
    base = pl.multiple_of(ka * half, 16)
    own = pl.ds(base, half)

    load = pltpu.make_async_copy(u_ref, g1_ref, u_sem)
    load.start()
    barrier = pltpu.get_barrier_semaphore()
    pl.semaphore_signal(barrier, inc=1, device_id=other, device_id_type=MESH)
    pl.semaphore_wait(barrier, 1)

    def exchange(ref, send, recv, step):
        at = ref.at[own, pl.ds(pl.multiple_of(step * columns, columns), columns)]
        return pltpu.make_async_remote_copy(
            src_ref=at,
            dst_ref=at,
            send_sem=send.at[step],
            recv_sem=recv.at[step],
            device_id=other,
            device_id_type=MESH,
        )

    def loop_columns(body):
        @pl.loop(0, steps)
        def _(j):
            body(j, pl.ds(pl.multiple_of(j * columns, columns), columns), j * columns)

    load.wait()

    @pl.loop(0, steps)
    def _(i):
        above = pl.ds(pl.multiple_of(i * columns, columns), columns)

        @pl.loop(i, steps)
        def _(j):
            left = pl.ds(pl.multiple_of(j * columns, columns), columns)
            value = g1_ref[above, left].astype(jnp.float32) + g1_ref[left, above].astype(jnp.float32).T
            g_ref[above, left] = value.astype(jnp.bfloat16)
            g_ref[left, above] = value.T.astype(jnp.bfloat16)

    def tile_p0(j, cols, start):
        square = jnp.dot(g_ref[own, :], g_ref[:, cols], preferred_element_type=jnp.float32)
        value = CUBIC_COEF * g_ref[own, cols].astype(jnp.float32) + QUINTIC_COEF * square
        p_ref[own, cols] = shifted(value, LINEAR_COEF, base, start).astype(jnp.bfloat16)
        exchange(p_ref, p_send, p_recv, j).start()

    loop_columns(tile_p0)
    for j in range(steps):
        exchange(p_ref, p_send, p_recv, j).wait()

    def tile_b(j, cols, start):
        value = jnp.dot(g_ref[own, :], p_ref[:, cols], preferred_element_type=jnp.float32)
        b_ref[:, cols] = value.astype(jnp.bfloat16)

    loop_columns(tile_b)

    def tile_g1(j, cols, start):
        value = jnp.dot(b_ref[...], p_ref[:, cols], preferred_element_type=jnp.float32)
        g1_ref[own, cols] = value.astype(jnp.bfloat16)
        exchange(g1_ref, g_send, g_recv, j).start()

    loop_columns(tile_g1)
    for j in range(steps):
        exchange(g1_ref, g_send, g_recv, j).wait()

    part = mine // 2
    first = pl.multiple_of(lax.axis_index("row") * mine + ka * part, 16)

    def tile_p1(j, cols, start):
        square = jnp.dot(g1_ref[pl.ds(first, part), :], g1_ref[:, cols], preferred_element_type=jnp.float32)
        value = CUBIC_COEF * g1_ref[pl.ds(first, part), cols].astype(jnp.float32) + QUINTIC_COEF * square
        p1_ref[:, cols] = shifted(value, LINEAR_COEF, first, start).astype(jnp.bfloat16)

    loop_columns(tile_p1)

    here = pl.ds(pl.multiple_of(ka * part, 16), part)

    def tile_q(j, cols, start):
        value = jnp.dot(p1_ref[...], p_ref[:, cols], preferred_element_type=jnp.float32)
        q_ref[here, cols] = value.astype(jnp.bfloat16)

    loop_columns(tile_q)
    copy = pltpu.make_async_remote_copy(
        src_ref=q_ref.at[here, :],
        dst_ref=q_ref.at[here, :],
        send_sem=q_sems.at[0],
        recv_sem=q_sems.at[1],
        device_id=other,
        device_id_type=MESH,
    )
    copy.start()
    copy.wait()


def polynomial(share, mine):
    n = share.shape[0]
    half = n // 2
    steps = n // tile_of(n, 256)
    dma = pltpu.SemaphoreType.DMA
    return pl.pallas_call(
        functools.partial(polynomial_kernel, mine),
        out_shape=jax.ShapeDtypeStruct((mine, n), jnp.bfloat16),
        in_specs=[pl.BlockSpec(memory_space=pl.ANY)],
        out_specs=pl.BlockSpec(memory_space=pltpu.VMEM),
        scratch_shapes=[
            pltpu.VMEM((n, n), jnp.bfloat16),
            pltpu.VMEM((n, n), jnp.bfloat16),
            pltpu.VMEM((n, n), jnp.bfloat16),
            pltpu.VMEM((half, n), jnp.bfloat16),
            pltpu.VMEM((mine // 2, n), jnp.bfloat16),
            dma,
            dma((steps,)),
            dma((steps,)),
            dma((steps,)),
            dma((steps,)),
            dma((2,)),
        ],
        compiler_params=pltpu.CompilerParams(
            collective_id=0, has_side_effects=True, vmem_limit_bytes=60 * 1024 * 1024
        ),
        cost_estimate=pl.CostEstimate(
            flops=2 * n * n * (3 * half + mine), bytes_accessed=2 * n * (n + mine), transcendentals=0
        ),
        name="polynomial",
    )(share)


def rows_dot(left, right):
    return lax.dot_general(left, right, (((1,), (1,)), ((), ())), preferred_element_type=jnp.float32)


def body(scale, count, iterate):
    mine, width = iterate.shape
    n = mine * count
    middle = count // 2
    z = lax.axis_index("row")
    upper = z >= middle

    def from_ahead(value, distance):
        return lax.ppermute(value, "row", [((i + distance) % count, i) for i in range(count)])

    rounded = iterate.astype(jnp.bfloat16)
    low, high = rounded[:, : width // 2], rounded[:, width // 2 :]
    ahead = [from_ahead(rounded, d) for d in range(1, middle)]
    far = from_ahead(jnp.where(upper, low, high), middle)
    strip = [0.5 * rows_dot(rounded, rounded)]
    strip += [rows_dot(rounded, block) for block in ahead]
    strip.append(rows_dot(jnp.where(upper, high, low), far))
    partial = jnp.concatenate([part.astype(jnp.bfloat16) for part in strip], axis=1)

    later, _ = lax.optimization_barrier((rounded, (ahead, far)))
    later_low, later_high = later[:, : width // 2], later[:, width // 2 :]
    far_rest = from_ahead(jnp.where(upper, later_high, later_low), middle)
    behind = [from_ahead(later, d) for d in range(middle + 1, count)]

    block = lax.psum_scatter(partial, ("col", "ka"), scatter_dimension=0, tiled=True)
    strips = lax.all_gather(block, ("row", "col", "ka"), axis=0, tiled=True)
    shares = []
    for i in range(count):
        share = jnp.pad(strips[i * mine : (i + 1) * mine], ((0, 0), (0, n - strips.shape[1])))
        shares.append(jnp.roll(share, i * mine, axis=1))
    share = jnp.concatenate(shares, axis=0)
    q = polynomial(share, mine)
    from_here = lax.dynamic_slice_in_dim(jnp.concatenate([q, q], axis=1), z * mine, n, axis=1)
    far_low, far_high = jnp.where(upper, far_rest, far), jnp.where(upper, far, far_rest)
    opposite = jnp.concatenate([far_low, far_high], axis=1)
    gathered = jnp.concatenate([rounded, *ahead, opposite, *behind], axis=0)
    update = jnp.dot(from_here, gathered, preferred_element_type=jnp.float32)
    return (scale * update).astype(jnp.bfloat16)


def solution(mesh):
    spec = P("row", ("col", "ka"))

    def whole(iterate):
        scale = math.sqrt(iterate.shape[1])
        return jax.shard_map(
            functools.partial(body, scale, mesh.shape["row"]), mesh=mesh, in_specs=(spec,), out_specs=spec, check_vma=False
        )(iterate)

    return whole
```

time: 916 us -> 506 us (0.55)
  waiting for transfers between devices: 818 us -> 295 us
  Pallas kernels: 0 us -> 93 us
  matrix products: 76.1 us -> 28.4 us
  other arithmetic: 7.72 us -> 53.6 us
  local copies, waits for them, and re-layouts: 0.01 us -> 13.2 us
    all_gather x6 -> x1, waiting for transfers between devices: 696 us -> 57.1 us  [body(): strips = lax.all_gather(block, ('row', 'col', 'ka'), axis=0, tiled=True)]
    ppermute x0 -> x4, waiting for transfers between devices: none -> 194 us  [from_ahead(): lax.ppermute(value, 'row', [((i + distance) % count, i) for i in range(co...]
    pallas_call x0 -> x1, Pallas kernels: none -> 93 us  [polynomial(): pl.pallas_call(functools.partial(polynomial_kernel, mine), out_shape=jax....]
    reduce_scatter x2 -> x1, waiting for transfers between devices: 123 us -> 44.4 us  [body(): lax.psum_scatter(partial, ('col', 'ka'), scatter_dimension=0, tiled=True)]
    dot_general x6 -> x4, matrix products: 76.1 us -> 28.4 us  [the longest x1 21.6 us: body(): update = jnp.dot(from_here, gathered, preferred_element_type=jnp.float32)]
    concatenate x0 -> x2, other arithmetic: none -> 47.1 us  [the longest x1 45.4 us: body(): share = jnp.concatenate(shares, axis=0)]
    slice x0 -> x5, local copies, waits for them, and re-layouts: none -> 13.2 us  [the longest x4 7.7 us: body(): shares.append(jnp.roll(share, i * mine, axis=1))]
  transfers between devices with their start and end apart: 8 -> 6, of which waited for: 8 -> 4; matrix products, arithmetic and copies ran while one was open for 0% -> 13% of each run, Pallas kernels for 0% -> 18%
where the time goes in v1:
time: 506 us
  waiting for transfers between devices  295 us (58%)
  Pallas kernels  93 us (18%)
  other arithmetic  53.6 us (11%)
  matrix products  28.4 us (6%)
  between operations  13.5 us (3%)
  local copies, waits for them, and re-layouts  13.2 us (3%)
  starting transfers between devices  9.12 us (2%)
    ppermute x4, waiting for transfers between devices, from_ahead(): lax.ppermute(value, 'row', [((i + distance) % count, i) for i in range(co...  194 us
    pallas_call x1, Pallas kernels, polynomial(): pl.pallas_call(functools.partial(polynomial_kernel, mine), out_shape=jax....  93 us
    all_gather x1, waiting for transfers between devices, body(): strips = lax.all_gather(block, ('row', 'col', 'ka'), axis=0, tiled=True)  57.1 us
    concatenate x1, other arithmetic, body(): share = jnp.concatenate(shares, axis=0)  45.4 us
    reduce_scatter x1, waiting for transfers between devices, body(): lax.psum_scatter(partial, ('col', 'ka'), scatter_dimension=0, tiled=True)  44.4 us
    dot_general x1, matrix products, body(): update = jnp.dot(from_here, gathered, preferred_element_type=jnp.float32)  21.6 us
  transfers between devices with their start and end apart: 6, of which 4 were waited for; matrix products, arithmetic and copies ran while one was open for 13% of the time, Pallas kernels for 18%

profile of v1, /device:TPU:0, one launch (start us, length us, event | category | flops | bytes accessed | tf_op | source)
XLA Modules:
  0.0 506.0 jit_solution(7758525271434045140)
XLA Ops:
  6.5 0.0 reduce-scatter.2.cloned.1.call-start
  6.5 2.5 convert_element_type.20
  9.0 5.1 %collective-permute-start = (bf16[640,1728]{0,1:T(8,128)(2,1)S(1)}, bf16[640,1728]{0,1:T(8,128)(2,1)}, u32[]{:S(2)}, u32[]{:S(2)}) collective-permute-start(bf16[640,1728]{0,1:T(8,128)(2,1)S(1)} %convert_element_type.20), channel_id=1, source_target_pairs={{8,0},{16,8},{24,16},{0,24},{9,1},{17,9},{25,17},{1,25},{10,2},{18... | collective-permute-start | bytes 6635528 | tf_op jit(solution)/shard_map/ppermute | solution.py:174
  14.1 0.1 broadcast_select_fusion.2
  14.2 0.1 collective-permute-start.1
  14.3 2.0 multiply_convert_fusion.1
  16.3 92.4 %collective-permute-done.1 = bf16[640,864]{0,1:T(8,128)(2,1)S(1)} collective-permute-done((bf16[640,864]{0,1:T(8,128)(2,1)S(1)}, bf16[640,864]{0,1:T(8,128)(2,1)S(1)}, u32[]{:S(2)}, u32[]{:S(2)}) %collective-permute-start.1) | collective-permute-done | bytes 1105952 | tf_op jit(solution)/shard_map/ppermute | solution.py:174
  108.8 1.2 convolution_convert_fusion
  109.9 0.0 collective-permute-done
  110.0 3.6 convolution_convert_fusion.1
  113.6 1.7 pad_maximum_fusion
  115.2 0.0 reduce-scatter.2.cloned.1.call-update
  115.3 0.0 all-gather.2.cloned.1.call-start
  115.3 44.4 %reduce-scatter.2.cloned.1.call-done = bf16[80,1920]{1,0:T(8,128)(2,1)} async-done(((bf16[640,1920]{1,0:T(8,128)(2,1)}), bf16[80,1920]{1,0:T(8,128)(2,1)}) %reduce-scatter.2.cloned.1.call-update) | async-done | bytes 307216 | tf_op jit(solution)/shard_map/reduce_scatter | solution.py:190
  159.7 0.0 all-gather.2.cloned.1.call-update
  159.7 1.1 slice_select_fusion
  160.8 2.4 collective-permute-start.2
  163.2 1.5 collective-permute-start.3
  164.8 101.2 %collective-permute-done.2 = bf16[640,864]{0,1:T(8,128)(2,1)} collective-permute-done((bf16[640,864]{0,1:T(8,128)(2,1)}, bf16[640,864]{0,1:T(8,128)(2,1)}, u32[]{:S(2)}, u32[]{:S(2)}) %collective-permute-start.2) | collective-permute-done | bytes 1105952 | tf_op jit(solution)/shard_map/ppermute | solution.py:174
  265.9 2.8 broadcast_select_fusion.1
  268.8 57.1 %all-gather.2.cloned.1.call-done = bf16[2560,1920]{1,0:T(8,128)(2,1)} async-done(((bf16[80,1920]{1,0:T(8,128)(2,1)}), bf16[2560,1920]{1,0:T(8,128)(2,1)}) %all-gather.2.cloned.1.call-update) | async-done | bytes 9830416 | tf_op jit(solution)/shard_map/all_gather | solution.py:191
  325.9 5.5 %fusion.26 = (bf16[640,1920]{1,0:T(8,128)(2,1)S(1)}, bf16[640,1920]{1,0:T(8,128)(2,1)S(1)}, bf16[640,1920]{1,0:T(8,128)(2,1)S(1)}, bf16[640,1920]{1,0:T(8,128)(2,1)}) fusion(bf16[2560,1920]{1,0:T(8,128)(2,1)} %all-gather.2.cloned.1.call-done), kind=kLoop, calls=%fused_computation.39 | loop fusion | bytes 19660800 | tf_op jit(solution)/shard_map/slice | solution.py:194
  331.4 1.6 pad_slice_fusion
  333.0 1.3 pad_slice_fusion.1
  334.3 2.7 slice.65
  337.0 2.1 slice.67
  339.1 45.4 %fusion.5.u_ref = bf16[2560,2560]{1,0:T(8,128)(2,1)} fusion(bf16[640,1920]{1,0:T(8,128)(2,1)S(1)} %get-tuple-element.9, bf16[640,1920]{1,0:T(8,128)(2,1)} %get-tuple-element.10, bf16[640,640]{1,0:T(8,128)(2,1)} %slice.67, bf16[640,1920]{1,0:T(8,128)(2,1)} %pad_slice_fusion, bf16[640,1280]{1,0:T(8,128)(2,1)} %slice.65, bf16[640,1280]{1,0:T(8,128)(2,1)} %pad_slice_fusion.1), kind=kLoop, calls=%fused_computation.8 | loop fusion | flops 117964800 | bytes 24576000 | tf_op jit(solution)/shard_map/concatenate | solution.py:196
  384.5 0.0 copy-start
  384.5 93.0 %polynomial.1 = bf16[640,2560]{1,0:T(8,128)(2,1)} custom-call(bf16[2560,2560]{1,0:T(8,128)(2,1)} %fusion.5.u_ref), custom_call_target="tpu_custom_call" | custom-call | flops 58720256000 | bytes 16384000 | tf_op jit(solution)/shard_map/polynomial/pallas_call | solution.py:134
  477.5 0.0 collective-permute-done.3
  477.5 0.0 copy-done
  477.5 21.6 %multiply_convert_fusion = bf16[640,1728]{0,1:T(8,128)(2,1)} fusion(bf16[640,1728]{0,1:T(8,128)(2,1)} %collective-permute-done.3, bf16[640,864]{0,1:T(8,128)(2,1)} %get-tuple-element.12, bf16[640,864]{0,1:T(8,128)(2,1)S(1)} %copy-done, bf16[640,1728]{0,1:T(8,128)(2,1)} %collective-permute-done, bf16[640,1728]{0,1:T(8,128)(2,1)S(1)} %convert_element_type.20, ...), kind=kOutput, calls=%fused_computation.21 | convolution fusion | flops 5715312640 | bytes 14336004 | tf_op jit(solution)/shard_map/dot_general | solution.py:202
Async XLA Ops:
  6.5 153.2 %reduce-scatter.2.cloned.1.call-start = ((), (), s32[]{:S(2)}) async-start(), calls=%async_computation.1 | async-start | bytes 2764800 | tf_op jit(solution)/shard_map/reduce_scatter | solution.py:190
  9.0 100.9 %collective-permute-start = (bf16[640,1728]{0,1:T(8,128)(2,1)S(1)}, bf16[640,1728]{0,1:T(8,128)(2,1)}, u32[]{:S(2)}, u32[]{:S(2)}) collective-permute-start(bf16[640,1728]{0,1:T(8,128)(2,1)S(1)} %convert_element_type.20), channel_id=1, source_target_pairs={{8,0},{16,8},{24,16},{0,24},{9,1},{17,9},{25,17},{1,25},{10,2},{18... | collective-permute-start | bytes 6635528 | tf_op jit(solution)/shard_map/ppermute | solution.py:174
  14.2 94.5 %collective-permute-start.1 = (bf16[640,864]{0,1:T(8,128)(2,1)S(1)}, bf16[640,864]{0,1:T(8,128)(2,1)S(1)}, u32[]{:S(2)}, u32[]{:S(2)}) collective-permute-start(bf16[640,864]{0,1:T(8,128)(2,1)S(1)} %broadcast_select_fusion.2), channel_id=1, source_target_pairs={{16,0},{24,8},{0,16},{8,24},{17,1},{25,9},{1,17},{9,25},{18,2},{26... | collective-permute-start | bytes 3317768 | tf_op jit(solution)/shard_map/ppermute | solution.py:174
  115.3 210.6 %all-gather.2.cloned.1.call-start = ((), (), s32[]{:S(2)}) async-start(), calls=%async_computation.2 | async-start | bytes 10137600 | tf_op jit(solution)/shard_map/all_gather | solution.py:191
  160.8 105.1 %collective-permute-start.2 = (bf16[640,864]{0,1:T(8,128)(2,1)}, bf16[640,864]{0,1:T(8,128)(2,1)}, u32[]{:S(2)}, u32[]{:S(2)}) collective-permute-start(bf16[640,864]{0,1:T(8,128)(2,1)} %slice_select_fusion), channel_id=1, source_target_pairs={{16,0},{24,8},{0,16},{8,24},{17,1},{25,9},{1,17},{9,25},{18,2},{26... | collective-permute-start | bytes 3317768 | tf_op jit(solution)/shard_map/ppermute | solution.py:174
  163.2 314.3 %collective-permute-start.3 = (bf16[640,1728]{0,1:T(8,128)(2,1)S(1)}, bf16[640,1728]{0,1:T(8,128)(2,1)}, u32[]{:S(2)}, u32[]{:S(2)}) collective-permute-start(bf16[640,1728]{0,1:T(8,128)(2,1)S(1)} %convert_element_type.20), channel_id=1, source_target_pairs={{24,0},{0,8},{8,16},{16,24},{25,1},{1,9},{9,17},{17,25},{26,2},{2,... | collective-permute-start | bytes 6635528 | tf_op jit(solution)/shard_map/ppermute | solution.py:174
  384.5 93.0 %copy-start = (bf16[640,864]{0,1:T(8,128)(2,1)S(1)}, bf16[640,864]{0,1:T(8,128)(2,1)}, u32[]{:S(2)}) copy-start(bf16[640,864]{0,1:T(8,128)(2,1)} %get-tuple-element.11) | copy-start | bytes 3317764
Sparse Core Ops, SparseCore 0:
  115.4 44.2 reduce-scatter.1
  162.6 163.2 all-gather.1

commit v2 on v1

--- a/solution.py
+++ b/solution.py
@@ -26,7 +26,8 @@
 
 
 def polynomial_kernel(
-    mine, u_ref, q_ref, g_ref, p_ref, g1_ref, b_ref, p1_ref, u_sem, p_send, p_recv, g_send, g_recv, q_sems
+    mine, packed, u_ref, x_ref, q_ref, behind_ref, g_ref, p_ref, g1_ref, b_ref, p1_ref, u_sem, x_send, x_recv,
+    p_send, p_recv, g_send, g_recv, q_sems
 ):
     n = g_ref.shape[0]
     half = n // 2
@@ -37,11 +38,45 @@
     base = pl.multiple_of(ka * half, 16)
     own = pl.ds(base, half)
 
-    load = pltpu.make_async_copy(u_ref, g1_ref, u_sem)
-    load.start()
+    loads = []
+    if packed:
+        count = n // mine
+        kept = u_ref.shape[1] // mine
+        for i in range(count):
+            for d in range(count):
+                j = (i + d) % count
+                at = g1_ref.at[i * mine : (i + 1) * mine, j * mine : (j + 1) * mine]
+                if d < kept:
+                    block = u_ref.at[i * mine : (i + 1) * mine, d * mine : (d + 1) * mine]
+                    loads.append(pltpu.make_async_copy(block, at, u_sem.at[i * kept + d]))
+                    loads[-1].start()
+                else:
+                    at[...] = jnp.zeros((mine, mine), jnp.bfloat16)
+    else:
+        loads.append(pltpu.make_async_copy(u_ref, g1_ref, u_sem.at[0]))
+        loads[-1].start()
     barrier = pltpu.get_barrier_semaphore()
     pl.semaphore_signal(barrier, inc=1, device_id=other, device_id_type=MESH)
-    pl.semaphore_wait(barrier, 1)
+    z, count, slots = lax.axis_index("row"), n // mine, behind_ref.shape[0]
+    targets = [{"row": lax.rem(z + s + 1, count)} for s in range(slots)]
+    sources = [{"row": lax.rem(z + count - s - 1, count)} for s in range(slots)]
+    for device in targets + sources:
+        pl.semaphore_signal(barrier, inc=1, device_id=device, device_id_type=MESH)
+    pl.semaphore_wait(barrier, 1 + 2 * slots)
+
+    sends = [
+        pltpu.make_async_remote_copy(
+            src_ref=x_ref,
+            dst_ref=behind_ref.at[s],
+            send_sem=x_send.at[s],
+            recv_sem=x_recv.at[s],
+            device_id=targets[s],
+            device_id_type=MESH,
+        )
+        for s in range(slots)
+    ]
+    for send in sends:
+        send.start()
 
     def exchange(ref, send, recv, step):
         at = ref.at[own, pl.ds(pl.multiple_of(step * columns, columns), columns)]
@@ -59,7 +94,8 @@
         def _(j):
             body(j, pl.ds(pl.multiple_of(j * columns, columns), columns), j * columns)
 
-    load.wait()
+    for load in loads:
+        load.wait()
 
     @pl.loop(0, steps)
     def _(i):
@@ -109,11 +145,21 @@
 
     here = pl.ds(pl.multiple_of(ka * part, 16), part)
 
-    def tile_q(j, cols, start):
-        value = jnp.dot(p1_ref[...], p_ref[:, cols], preferred_element_type=jnp.float32)
-        q_ref[here, cols] = value.astype(jnp.bfloat16)
-
-    loop_columns(tile_q)
+    if packed:
+
+        @pl.loop(0, n // mine)
+        def _(d):
+            source = lax.rem(lax.axis_index("row") + d, n // mine)
+            cols = pl.ds(pl.multiple_of(source * mine, 128), mine)
+            value = jnp.dot(p1_ref[...], p_ref[:, cols], preferred_element_type=jnp.float32)
+            q_ref[here, pl.ds(pl.multiple_of(d * mine, 128), mine)] = value.astype(jnp.bfloat16)
+    else:
+
+        def tile_q(j, cols, start):
+            value = jnp.dot(p1_ref[...], p_ref[:, cols], preferred_element_type=jnp.float32)
+            q_ref[here, cols] = value.astype(jnp.bfloat16)
+
+        loop_columns(tile_q)
     copy = pltpu.make_async_remote_copy(
         src_ref=q_ref.at[here, :],
         dst_ref=q_ref.at[here, :],
@@ -124,25 +170,34 @@
     )
     copy.start()
     copy.wait()
-
-
-def polynomial(share, mine):
+    for send in sends:
+        send.wait()
+
+
+def polynomial(share, turned, packed):
     n = share.shape[0]
+    width, mine = turned.shape
+    slots = n // mine - n // mine // 2 - 1
     half = n // 2
     steps = n // tile_of(n, 256)
     dma = pltpu.SemaphoreType.DMA
     return pl.pallas_call(
-        functools.partial(polynomial_kernel, mine),
-        out_shape=jax.ShapeDtypeStruct((mine, n), jnp.bfloat16),
-        in_specs=[pl.BlockSpec(memory_space=pl.ANY)],
-        out_specs=pl.BlockSpec(memory_space=pltpu.VMEM),
+        functools.partial(polynomial_kernel, mine, packed),
+        out_shape=(
+            jax.ShapeDtypeStruct((mine, n), jnp.bfloat16),
+            jax.ShapeDtypeStruct((slots, width, mine), jnp.bfloat16),
+        ),
+        in_specs=[pl.BlockSpec(memory_space=pl.ANY)] * 2,
+        out_specs=(pl.BlockSpec(memory_space=pltpu.VMEM), pl.BlockSpec(memory_space=pl.ANY)),
         scratch_shapes=[
             pltpu.VMEM((n, n), jnp.bfloat16),
             pltpu.VMEM((n, n), jnp.bfloat16),
             pltpu.VMEM((n, n), jnp.bfloat16),
             pltpu.VMEM((half, n), jnp.bfloat16),
             pltpu.VMEM((mine // 2, n), jnp.bfloat16),
-            dma,
+            dma(((n // mine) * (share.shape[1] // mine) if packed else 1,)),
+            dma((slots,)),
+            dma((slots,)),
             dma((steps,)),
             dma((steps,)),
             dma((steps,)),
@@ -156,7 +211,7 @@
             flops=2 * n * n * (3 * half + mine), bytes_accessed=2 * n * (n + mine), transcendentals=0
         ),
         name="polynomial",
-    )(share)
+    )(share, turned)
 
 
 def rows_dot(left, right):
@@ -185,21 +240,27 @@
     later, _ = lax.optimization_barrier((rounded, (ahead, far)))
     later_low, later_high = later[:, : width // 2], later[:, width // 2 :]
     far_rest = from_ahead(jnp.where(upper, later_high, later_low), middle)
-    behind = [from_ahead(later, d) for d in range(middle + 1, count)]
 
     block = lax.psum_scatter(partial, ("col", "ka"), scatter_dimension=0, tiled=True)
+    block, far_rest = lax.optimization_barrier((block, far_rest))
     strips = lax.all_gather(block, ("row", "col", "ka"), axis=0, tiled=True)
-    shares = []
-    for i in range(count):
-        share = jnp.pad(strips[i * mine : (i + 1) * mine], ((0, 0), (0, n - strips.shape[1])))
-        shares.append(jnp.roll(share, i * mine, axis=1))
-    share = jnp.concatenate(shares, axis=0)
-    q = polynomial(share, mine)
-    from_here = lax.dynamic_slice_in_dim(jnp.concatenate([q, q], axis=1), z * mine, n, axis=1)
+    packed = mine % 128 == 0
+    if packed:
+        q, behind = polynomial(strips, rounded.T, packed)
+    else:
+        shares = []
+        for i in range(count):
+            share = jnp.pad(strips[i * mine : (i + 1) * mine], ((0, 0), (0, n - strips.shape[1])))
+            shares.append(jnp.roll(share, i * mine, axis=1))
+        q, behind = polynomial(jnp.concatenate(shares, axis=0), rounded.T, packed)
+        q = lax.dynamic_slice_in_dim(jnp.concatenate([q, q], axis=1), z * mine, n, axis=1)
+
     far_low, far_high = jnp.where(upper, far_rest, far), jnp.where(upper, far, far_rest)
     opposite = jnp.concatenate([far_low, far_high], axis=1)
-    gathered = jnp.concatenate([rounded, *ahead, opposite, *behind], axis=0)
-    update = jnp.dot(from_here, gathered, preferred_element_type=jnp.float32)
+    blocks = [rounded, *ahead, opposite] + [behind[s].T for s in reversed(range(behind.shape[0]))]
+    update = 0.0
+    for d, rows in enumerate(blocks):
+        update += jnp.dot(q[:, d * mine : (d + 1) * mine], rows, preferred_element_type=jnp.float32)
     return (scale * update).astype(jnp.bfloat16)
 
 

time: 506 us -> 361 us (0.71)
  waiting for transfers between devices: 295 us -> 219 us
  other arithmetic: 53.6 us -> 10.8 us
  local copies, waits for them, and re-layouts: 13.2 us -> 0.02 us
  matrix products: 28.4 us -> 19.7 us
    ppermute x4 -> x3, waiting for transfers between devices: 194 us -> 142 us  [from_ahead(): lax.ppermute(value, 'row', [((i + distance) % count, i) for i in range(co...]
    concatenate x1 -> x0, other arithmetic: 45.4 us -> none  [body(): share = jnp.concatenate(shares, axis=0)]
    reduce_scatter x1, waiting for transfers between devices: 44.4 us -> 0.01 us  [body(): lax.psum_scatter(partial, ('col', 'ka'), scatter_dimension=0, tiled=True)]
    all_gather x1, waiting for transfers between devices: 57.1 us -> 76.4 us  [body(): strips = lax.all_gather(block, ('row', 'col', 'ka'), axis=0, tiled=True)]
    slice x5 -> x0, local copies, waits for them, and re-layouts: 13.2 us -> none  [the longest x4 7.7 us: body(): shares.append(jnp.roll(share, i * mine, axis=1))]
    dot_general x1 -> x4, matrix products: 21.6 us -> 12.9 us  [body(): jnp.dot(q[:, d * mine:(d + 1) * mine], rows, preferred_element_type=jnp.f...]
  transfers between devices with their start and end apart: 6 -> 5, of which waited for: 4 -> 3; matrix products, arithmetic and copies ran while one was open for 13% -> 3% of each run, Pallas kernels for 18% -> 0%
where the time goes in v2:
time: 361 us
  waiting for transfers between devices  219 us (61%)
  Pallas kernels  92.3 us (26%)
  matrix products  19.7 us (5%)
  between operations  13.6 us (4%)
  other arithmetic  10.8 us (3%)
  starting transfers between devices  5.47 us (2%)
    ppermute x3, waiting for transfers between devices, from_ahead(): lax.ppermute(value, 'row', [((i + distance) % count, i) for i in range(co...  142 us
    pallas_call x1, Pallas kernels, polynomial(): pl.pallas_call(functools.partial(polynomial_kernel, mine, packed), out_sh...  92.3 us
    all_gather x1, waiting for transfers between devices, body(): strips = lax.all_gather(block, ('row', 'col', 'ka'), axis=0, tiled=True)  76.4 us
    dot_general x4, matrix products, body(): jnp.dot(q[:, d * mine:(d + 1) * mine], rows, preferred_element_type=jnp.f...  12.9 us
  transfers between devices with their start and end apart: 5, of which 3 were waited for; matrix products, arithmetic and copies ran while one was open for 3% of the time, Pallas kernels for 0%

profile of v2, /device:TPU:0, one launch (start us, length us, event | category | flops | bytes accessed | tf_op | source)
XLA Modules:
  0.0 360.6 jit_solution(16121182995394751235)
XLA Ops:
  6.5 0.0 reduce-scatter.2.cloned.1.call-start
  6.5 2.5 convert_element_type.15
  9.0 5.1 %collective-permute-start = (bf16[640,1728]{0,1:T(8,128)(2,1)S(1)}, bf16[640,1728]{0,1:T(8,128)(2,1)}, u32[]{:S(2)}, u32[]{:S(2)}) collective-permute-start(bf16[640,1728]{0,1:T(8,128)(2,1)S(1)} %convert_element_type.15), channel_id=1, source_target_pairs={{8,0},{16,8},{24,16},{0,24},{9,1},{17,9},{25,17},{1,25},{10,2},{18... | collective-permute-start | bytes 6635528 | tf_op jit(solution)/shard_map/ppermute | solution.py:229
  14.1 0.1 broadcast_select_fusion.2
  14.2 0.1 collective-permute-start.1
  14.3 2.0 multiply_convert_fusion.1
  16.3 92.4 %collective-permute-done.1 = bf16[640,864]{0,1:T(8,128)(2,1)S(1)} collective-permute-done((bf16[640,864]{0,1:T(8,128)(2,1)S(1)}, bf16[640,864]{0,1:T(8,128)(2,1)S(1)}, u32[]{:S(2)}, u32[]{:S(2)}) %collective-permute-start.1) | collective-permute-done | bytes 1105952 | tf_op jit(solution)/shard_map/ppermute | solution.py:229
  108.8 1.2 convolution_convert_fusion
  110.0 0.0 copy-done.1
  110.0 0.0 collective-permute-done
  110.0 3.6 %convolution_convert_fusion.1 = bf16[640,640]{1,0:T(8,128)(2,1)S(1)} fusion(bf16[640,1728]{0,1:T(8,128)(2,1)S(1)} %convert_element_type.15, bf16[640,1728]{0,1:T(8,128)(2,1)} %collective-permute-done), kind=kOutput, calls=%fused_computation.9 | convolution fusion | flops 1415987200 | bytes 5242880 | tf_op jit(solution)/shard_map/dot_general | solution.py:218
  113.6 1.6 pad_maximum_fusion
  115.3 0.0 reduce-scatter.2.cloned.1.call-update
  115.3 0.2 all-gather.2.cloned.1.call-start
  115.5 0.1 slice_select_fusion
  115.6 0.1 collective-permute-start.2
  115.7 49.9 %collective-permute-done.2 = bf16[640,864]{0,1:T(8,128)(2,1)} collective-permute-done((bf16[640,864]{0,1:T(8,128)(2,1)S(1)}, bf16[640,864]{0,1:T(8,128)(2,1)}, u32[]{:S(2)}, u32[]{:S(2)}) %collective-permute-start.2) | collective-permute-done | bytes 1105952 | tf_op jit(solution)/shard_map/ppermute | solution.py:229
  165.7 0.0 all-gather.2.cloned.1.call-update
  165.7 0.0 copy-start.2
  165.7 3.9 %convert_bitcast_fusion.x_ref = bf16[1728,640]{1,0:T(8,128)(2,1)} fusion(f32[640,1728]{0,1:T(8,128)} %param.1), kind=kLoop, calls=%fused_computation.25 | loop fusion | flops 1105920 | bytes 6635520 | tf_op jit(solution)/shard_map/transpose | solution.py:249
  169.6 0.0 copy-done.2
  169.6 2.5 broadcast_select_fusion.1
  172.1 76.4 %all-gather.2.cloned.1.call-done.u_ref = bf16[2560,1920]{1,0:T(8,128)(2,1)} async-done(((bf16[80,1920]{1,0:T(8,128)(2,1)}), bf16[2560,1920]{1,0:T(8,128)(2,1)}) %all-gather.2.cloned.1.call-update) | async-done | bytes 9830416 | tf_op jit(solution)/shard_map/all_gather | solution.py:246
  248.5 92.3 %polynomial.1 = (bf16[640,2560]{1,0:T(8,128)(2,1)}, bf16[1,1728,640]{2,1,0:T(8,128)(2,1)}) custom-call(bf16[2560,1920]{1,0:T(8,128)(2,1)} %all-gather.2.cloned.1.call-done.u_ref, bf16[1728,640]{1,0:T(8,128)(2,1)} %convert_bitcast_fusion.x_ref), custom_call_target="tpu_custom_call" | custom-call | flops 58720256000 | bytes 16384000 | tf_op jit(solution)/shard_map/polynomial/pallas_call | solution.py:184
  340.8 0.0 copy-start.3
  340.8 0.0 copy-start.4
  340.8 3.4 fusion.13
  344.2 0.0 copy-done.3
  344.2 0.0 copy-done.4
  344.3 2.1 fusion.3
  346.4 3.8 %fusion.11 = f32[640,1728]{0,1:T(8,128)S(1)} fusion(bf16[640,1728]{0,1:T(8,128)(2,1)} %collective-permute-done, bf16[640,2560]{1,0:T(8,128)(2,1)S(1)} %copy-done.3), kind=kOutput, calls=%fused_computation.20 | convolution fusion | flops 1415577600 | bytes 7454720 | tf_op jit(solution)/shard_map/dot_general | solution.py:263
  350.2 3.5 multiply_convert_fusion
  (4 shorter events, 0.0 us)
Async XLA Ops:
  6.5 159.1 %reduce-scatter.2.cloned.1.call-start = ((), (), s32[]{:S(2)}) async-start(), calls=%async_computation.1 | async-start | bytes 2764800 | tf_op jit(solution)/shard_map/reduce_scatter | solution.py:244
  9.0 101.0 %collective-permute-start = (bf16[640,1728]{0,1:T(8,128)(2,1)S(1)}, bf16[640,1728]{0,1:T(8,128)(2,1)}, u32[]{:S(2)}, u32[]{:S(2)}) collective-permute-start(bf16[640,1728]{0,1:T(8,128)(2,1)S(1)} %convert_element_type.15), channel_id=1, source_target_pairs={{8,0},{16,8},{24,16},{0,24},{9,1},{17,9},{25,17},{1,25},{10,2},{18... | collective-permute-start | bytes 6635528 | tf_op jit(solution)/shard_map/ppermute | solution.py:229
  14.2 94.5 %collective-permute-start.1 = (bf16[640,864]{0,1:T(8,128)(2,1)S(1)}, bf16[640,864]{0,1:T(8,128)(2,1)S(1)}, u32[]{:S(2)}, u32[]{:S(2)}) collective-permute-start(bf16[640,864]{0,1:T(8,128)(2,1)S(1)} %broadcast_select_fusion.2), channel_id=1, source_target_pairs={{16,0},{24,8},{0,16},{8,24},{17,1},{25,9},{1,17},{9,25},{18,2},{26... | collective-permute-start | bytes 3317768 | tf_op jit(solution)/shard_map/ppermute | solution.py:229
  108.8 1.2 copy-start.1
  115.3 133.2 %all-gather.2.cloned.1.call-start = ((), (), s32[]{:S(2)}) async-start(), calls=%async_computation.2 | async-start | bytes 10137600 | tf_op jit(solution)/shard_map/all_gather | solution.py:246
  115.6 50.0 %collective-permute-start.2 = (bf16[640,864]{0,1:T(8,128)(2,1)S(1)}, bf16[640,864]{0,1:T(8,128)(2,1)}, u32[]{:S(2)}, u32[]{:S(2)}) collective-permute-start(bf16[640,864]{0,1:T(8,128)(2,1)S(1)} %slice_select_fusion), channel_id=1, source_target_pairs={{16,0},{24,8},{0,16},{8,24},{17,1},{25,9},{1,17},{9,25},{18,2},{26... | collective-permute-start | bytes 3317768 | tf_op jit(solution)/shard_map/ppermute | solution.py:229
  165.7 3.9 %copy-start.2 = (bf16[640,864]{0,1:T(8,128)(2,1)S(1)}, bf16[640,864]{0,1:T(8,128)(2,1)}, u32[]{:S(2)}) copy-start(bf16[640,864]{0,1:T(8,128)(2,1)} %copy-done.1) | copy-start | bytes 3317764
  340.8 3.5 copy-start.3
  340.8 3.5 copy-start.4
  346.4 3.9 %copy-start = (bf16[640,864]{0,1:T(8,128)(2,1)S(1)}, bf16[640,864]{0,1:T(8,128)(2,1)}, u32[]{:S(2)}) copy-start(bf16[640,864]{0,1:T(8,128)(2,1)} %get-tuple-element.16) | copy-start | bytes 3317764
Sparse Core Ops, SparseCore 0:
  115.4 44.3 reduce-scatter.1
  165.8 82.6 all-gather.1
